TPU v7x, 512 devices: a whole 4x4x16 slice. The times are simulated.
512 devices in a mesh: dp: 64 (over x, z_hi, y), tensor: 8 (over z_lo, core).
Axes of the slice: x: 4, y: 4, z: 16 (z_hi: 4, z_lo: 4; z = z_hi * 4 + z_lo), core: 2. Of those that a mesh axis runs over, the one named last changes fastest.
Arguments:
- tokens: bfloat16 [1280, 6144], P('dp', 'tensor'), may hold values from -6 to 6
- route_ids: int32 [1280, 2], replicated, may hold values from 0 to 3, all different within a row
- route_probs: bfloat16 [1280, 2], replicated, may hold values from 0.099609375 to 1
- w_gate: bfloat16 [4, 6144, 8192], P(None, 'tensor', 'dp'), may hold values from -0.078125 to 0.078125
- w_up: bfloat16 [4, 6144, 8192], P(None, 'tensor', 'dp'), may hold values from -0.078125 to 0.078125
- w_down: bfloat16 [4, 8192, 6144], P(None, 'dp', 'tensor'), may hold values from -0.0625 to 0.0625
Outputs:
- mixed_out: bfloat16 [1280, 6144], P('dp', 'tensor')
Inputs may be any that keep to these rules, and one draw needn't show every extreme that they name: `route_ids`: each row names 2 different experts, and every expert is named by some row.
All inputs are finite; a program needn't handle non-finite values.
Results may differ from a plain program's by a relative error of at most 0.0049.
Values may be sent and summed in bfloat16 or wider, within the bound.
A program may use at most 64 MiB of HBM per device.

v0:
```python
import jax
import jax.numpy as jnp
from jax import lax
from jax.sharding import Mesh
from jax.sharding import PartitionSpec as P

BLOCK = 128
DP = ("dp_0", "dp_1", "dp_2")


def in_one_piece(arrays, axis, split_dim, concat_dim, along):
    widths = [a.shape[along] for a in arrays]
    both = jnp.concatenate(arrays, axis=along)
    result = lax.all_to_all(both, axis, split_axis=split_dim, concat_axis=concat_dim, tiled=True)
    return tuple(jnp.split(result, [sum(widths[:k]) for k in range(1, len(widths))], axis=along))


def from_everyone(x, axis):
    peers = lax.axis_size(axis)
    return lax.all_to_all(jnp.broadcast_to(x[None], (peers, *x.shape)), axis, 0, 0, tiled=True)


def laid_out(parts, dim):
    shape = list(parts.shape[1:])
    shape[dim] *= parts.shape[0]
    return jnp.moveaxis(parts, 0, dim).reshape(shape)


def gathered_copies(x, axis, dim):
    parts = from_everyone(x, axis)
    return laid_out(parts, dim)


def own_block(parts, axes, sequence):
    inside = parts.shape[1:]
    parts = parts.reshape(*(lax.axis_size(a) for a in axes), *inside)
    parts = jnp.moveaxis(parts, sequence, range(len(axes))).reshape(-1, *inside)
    for k in sequence:
        parts = lax.psum_scatter(parts, axes[k], scatter_dimension=0, tiled=True)
    return parts[0]


def split_up(x, dim, peers):
    before, after = (x.shape[:dim], x.shape[dim + 1 :])
    return jnp.moveaxis(x.reshape(*before, peers, -1, *after), dim, 0)


def sum_by_axis(x, axes, sequence, dim):
    peers = lax.axis_size(axes)
    return own_block(split_up(x, dim, peers), axes, sequence)


def local(tokens, route_ids, route_probs, w_gate, w_up, w_down):
    all_tokens = lax.all_gather(tokens, DP, axis=0, tiled=True)
    token_count, top_count = route_ids.shape
    expert_count, model_width, hidden_width = w_gate.shape
    out_width = w_down.shape[2]
    pair_count = token_count * top_count
    block_count = pair_count // BLOCK + expert_count
    row_count = block_count * BLOCK
    flat_ids = route_ids.reshape(pair_count)
    expert_range = jnp.arange(expert_count, dtype=jnp.int32)
    member = (flat_ids[:, None] == expert_range[None, :]).astype(jnp.int32)
    counts = jnp.sum(member, axis=0)
    block_sizes = (counts + BLOCK - 1) // BLOCK
    block_ends = jnp.cumsum(block_sizes)
    block_starts = block_ends - block_sizes
    earlier = jnp.cumsum(member, axis=0) - member
    within = jnp.sum(earlier * member, axis=1)
    slot_index = jnp.sum(member * block_starts[None, :], axis=1) * BLOCK + within
    pair_token = jnp.arange(pair_count, dtype=jnp.int32) // top_count
    source_row = jnp.full((row_count,), token_count, jnp.int32).at[slot_index].set(pair_token)
    block_range = jnp.arange(block_count, dtype=jnp.int32)
    block_expert = jnp.sum((block_range[:, None] >= block_ends[None, :]).astype(jnp.int32), axis=1)
    block_expert = jnp.minimum(block_expert, expert_count - 1)
    pair_weight = route_probs.astype(jnp.float32).reshape(pair_count)
    slot_weight = jnp.zeros((row_count,), jnp.float32).at[slot_index].set(pair_weight)
    zero_row = jnp.zeros((1, model_width), jnp.bfloat16)
    padded_tokens = jnp.concatenate([all_tokens, zero_row], axis=0)
    token_blocks = padded_tokens[source_row].reshape(block_count, BLOCK, model_width)

    def first_pass(carry, items):
        block_tokens, expert = items
        gate_weight = lax.dynamic_index_in_dim(w_gate, expert, 0, keepdims=False)
        up_weight = lax.dynamic_index_in_dim(w_up, expert, 0, keepdims=False)
        gate_block = jnp.dot(block_tokens, gate_weight, preferred_element_type=jnp.float32)
        up_block = jnp.dot(block_tokens, up_weight, preferred_element_type=jnp.float32)
        return (carry, (gate_block, up_block))

    unused, (gate_part, up_part) = lax.scan(first_pass, 0, (token_blocks, block_expert))
    gate_part = gate_part.reshape(row_count, hidden_width)
    up_part = up_part.reshape(row_count, hidden_width)
    gate_terms, up_terms = in_one_piece((gate_part[None], up_part[None]), "tensor", 1, 0, 2)
    gate_sum = jnp.sum(gate_terms, axis=0)
    up_sum = jnp.sum(up_terms, axis=0)
    hidden_share = (gate_sum * jax.nn.sigmoid(gate_sum) * up_sum).astype(jnp.bfloat16)
    hidden = gathered_copies(hidden_share, "tensor", 0)
    hidden_blocks = hidden.reshape(block_count, BLOCK, hidden_width)
    source_blocks = source_row.reshape(block_count, BLOCK)
    weight_blocks = slot_weight.reshape(block_count, BLOCK)

    def second_pass(mixed_acc, items):
        block_hidden, block_source, block_weight, expert = items
        down_weight = lax.dynamic_index_in_dim(w_down, expert, 0, keepdims=False)
        out_block = jnp.dot(block_hidden, down_weight, preferred_element_type=jnp.float32)
        mixed_acc = mixed_acc.at[block_source].add(out_block * block_weight[:, None])
        return (mixed_acc, 0)

    start_acc = jnp.zeros((token_count + 1, out_width), jnp.float32)
    mixed_acc, unused = lax.scan(
        second_pass, start_acc, (hidden_blocks, source_blocks, weight_blocks, block_expert)
    )
    mixed_part = mixed_acc[:token_count]
    return sum_by_axis(mixed_part, DP, (0, 2, 1), 0).astype(jnp.bfloat16)


def solution(mesh):
    torus = Mesh(
        mesh.devices.reshape(4, 4, 4, mesh.shape["tensor"]), ("dp_0", "dp_1", "dp_2", "tensor")
    )
    in_specs = (
        P(DP, "tensor"),
        P(),
        P(),
        P(None, "tensor", DP),
        P(None, "tensor", DP),
        P(None, DP, "tensor"),
    )
    out_specs = P(DP, "tensor")
    return jax.shard_map(local, mesh=torus, in_specs=in_specs, out_specs=out_specs, check_vma=False)
```

profile of v0, /device:TPU:1, one launch (start us, length us, event | category | flops | bytes accessed | tf_op | source)
XLA Modules:
  0.0 801.5 jit_solution(947273861664436097)
XLA Ops:
  11.1 9.9 %scatter_custom_fusion.1 = s32[3072]{0:T(1024)S(1)} fusion(s32[2560]{0:T(1024)S(1)} %fusion.28, s32[2560]{0:T(1024)S(1)} %add_select_fusion, s32[]{:T(128)} %constant.90.clone.1), kind=kCustom, calls=%fused_computation.61 | custom fusion | bytes 12292 | tf_op jit(solution)/shard_map/scatter | solution.py:72
  21.7 111.1 %all-gather.3.cloned.1.call-done = bf16[64,20,768]{2,1,0:T(8,128)(2,1)} async-done(((bf16[1,20,768]{2,1,0:T(8,128)(2,1)}), bf16[64,20,768]{2,1,0:T(8,128)(2,1)}) %all-gather.3.cloned.1.call-update) | async-done | bytes 1966096 | tf_op jit(solution)/shard_map/all_gather | solution.py:54
  138.4 14.5 %gather_fusion = bf16[3072,768]{1,0:T(8,128)(2,1)} fusion(bf16[1281,768]{1,0:T(8,128)(2,1)S(1)} %concatenate.6, s32[3072]{0:T(1024)} %fusion.26), kind=kCustom, calls=%fused_computation | custom fusion | bytes 9449472 | tf_op jit(solution)/shard_map/gather | solution.py:80
  153.0 134.4 %while.22 = (s32[]{:T(128)}, f32[24,128,128]{2,1,0:T(8,128)S(1)}, f32[24,128,128]{2,1,0:T(8,128)}, bf16[24,128,768]{2,1,0:T(8,128)(2,1)}, s32[24]{0:T(128)S(1)},...) while((s32[]{:T(128)}, f32[24,128,128]{2,1,0:T(8,128)S(1)}, ...), condition=%wide.region_9.10_spmd, body=%wide.region_8.9_spmd.sunk | while | flops 50331652 | bytes 919707 | solution.py:90
  292.2 75.2 %all_to_all.17 = f32[1,3072,256]{2,0,1:T(1,128)S(1)} all-to-all(f32[1,3072,256]{2,0,1:T(1,128)S(1)} %pad_maximum_fusion), channel_id=1, replica_groups=mesh['dp_0'=4,'dp_1'=4,'dp_2'=4,'tensor'=8] {'tensor'}, dimensions={1} | all-to-all | bytes 6291456 | tf_op jit(solution)/shard_map/all_to_all | solution.py:14
  373.8 10.1 %scatter_custom_fusion.2 = f32[3072]{0:T(1024)S(1)} fusion(s32[2560]{0:T(1024)} %copy-done.1, f32[2560]{0:T(1024)S(1)} %reshape.235, f32[]{:T(128)} %constant.88.clone.1), kind=kCustom, calls=%fused_computation.59 | custom fusion | bytes 12800 | tf_op jit(solution)/shard_map/scatter | solution.py:77
  383.9 9.5 %all-to-all-done.1 = bf16[8,384,128]{2,1,0:T(8,128)(2,1)S(1)} async-done(((bf16[8,384,128]{2,1,0:T(8,128)(2,1)}), bf16[8,384,128]{2,1,0:T(8,128)(2,1)S(1)}, u32[]{:S(2)}, u32[]{:S(2)}) %all-to-all-start.1) | async-done | bytes 786464 | tf_op jit(solution)/shard_map/all_to_all | solution.py:20
  395.6 231.8 %while.23 = (s32[]{:T(128)}, f32[1281,768]{1,0:T(8,128)}, s32[24,128]{1,0:T(8,128)}, bf16[24,128,128]{2,1,0:T(8,128)(2,1)S(1)}, s32[24]{0:T(128)S(1)}, /*index=5...) while((s32[]{:T(128)}, f32[1281,768]{1,0:T(8,128)}, ...), condition=%wide.region_15.16_spmd, body=%wide.region_13.15_spmd.sunk | while | flops 25362820 | bytes 1805983 | solution.py:110
  399.9 5.3 scatter_fusion
  409.5 5.3 scatter_fusion
  419.2 5.3 scatter_fusion
  428.8 5.3 scatter_fusion
  438.4 5.4 scatter_fusion
  448.1 5.3 scatter_fusion
  457.8 5.3 scatter_fusion
  467.4 5.3 scatter_fusion
  477.1 5.3 scatter_fusion
  486.7 5.4 scatter_fusion
  496.4 5.3 scatter_fusion
  506.0 5.3 scatter_fusion
  515.6 5.3 scatter_fusion
  544.6 5.4 scatter_fusion
  554.3 5.3 scatter_fusion
  573.6 5.3 scatter_fusion
  583.2 5.3 scatter_fusion
  602.5 5.4 scatter_fusion
  612.2 5.4 scatter_fusion
  621.9 5.4 scatter_fusion
  636.4 6.8 copy.27
  648.5 48.0 %reduce-scatter.4.cloned.1.call-done = f32[16,20,768]{2,0,1:T(8,128)} async-done(((f32[64,20,768]{2,0,1:T(8,128)}), f32[16,20,768]{2,0,1:T(8,128)}) %reduce-scatter.4.cloned.1.call-update) | async-done | bytes 983056 | tf_op jit(solution)/shard_map/reduce_scatter | solution.py:39
  699.7 58.1 %all-reduce.6.cloned.1.call-done = f32[16,20,768]{2,0,1:T(8,128)} async-done(((f32[16,20,768]{2,0,1:T(8,128)}), f32[16,20,768]{2,0,1:T(8,128)}) %all-reduce.6.cloned.1.call-update) | async-done | bytes 983056
  758.9 34.7 %all-reduce.7 = bf16[4,20,768]{2,0,1:T(4,128)(2,1)S(1)} all-reduce(f32[4,20,768]{2,0,1:T(4,128)S(1)} %constant_dynamic-slice_fusion.3), channel_id=4, replica_groups=mesh['dp_0'=4,'dp_1'=4,'dp_2'=4,'tensor'=8] {'dp_1'}, use_global_device_ids=true, to_apply=%region_18.19.clone | all-reduce | flops 61440 | bytes 368640
  (224 shorter events, 211.7 us)
Async XLA Ops:
  6.5 126.3 %all-gather.3.cloned.1.call-start = ((), (), s32[]{:S(2)}) async-start(), calls=%async_computation.4 | async-start | bytes 2396160 | tf_op jit(solution)/shard_map/all_gather | solution.py:54
  11.1 121.8 %copy-start.1 = (s32[2560]{0:T(1024)}, s32[2560]{0:T(1024)S(1)}, u32[]{:S(2)}) copy-start(s32[2560]{0:T(1024)S(1)} %fusion.28) | copy-start | bytes 30724
  21.0 111.8 %copy-start = (s32[3072]{0:T(1024)}, s32[3072]{0:T(1024)S(1)}, u32[]{:S(2)}) copy-start(s32[3072]{0:T(1024)S(1)} %scatter_custom_fusion.1) | copy-start | bytes 36868
  367.6 5.7 copy-start.2
  368.8 24.6 %all-to-all-start.1 = ((bf16[8,384,128]{2,1,0:T(8,128)(2,1)}), bf16[8,384,128]{2,1,0:T(8,128)(2,1)S(1)}, u32[]{:S(2)}, u32[]{:S(2)}) async-start(bf16[8,384,128]{2,1,0:T(8,128)(2,1)} %broadcast_in_dim.37), calls=%async_computation.1 | async-start | bytes 1572864 | tf_op jit(solution)/shard_map/all_to_all | solution.py:20
  373.3 323.2 %reduce-scatter.4.cloned.1.call-start = ((), (), s32[]{:S(2)}) async-start(), calls=%async_computation.3 | async-start | bytes 4915200 | tf_op jit(solution)/shard_map/reduce_scatter | solution.py:39
  648.4 109.4 %all-reduce.6.cloned.1.call-start = ((), (), s32[]{:S(2)}) async-start(), calls=%async_computation.5 | async-start | bytes 1966080
Sparse Core Ops, SparseCore 0:
  11.4 121.3 all-gather.2
  648.5 47.8 reduce-scatter.3
  698.9 58.9 all-reduce.5
where the time goes:
time: 810 us; the launch traced here: 802 us
  waiting for transfers between devices  227 us (28%)
  other arithmetic  153 us (19%)
  blocking collectives  110 us (14%)
  local copies, waits for them, and re-layouts  102 us (13%)
  matrix products  100 us (12%)
  loops' own time  90.8 us (11%)
  between operations  13.9 us (2%)
    scatter-add x24, other arithmetic, second_pass(): mixed_acc.at[block_source].add(out_block * block_weight[:, None])  129 us
    all_gather x1, waiting for transfers between devices, local(): all_tokens = lax.all_gather(tokens, DP, axis=0, tiled=True)  111 us
    all_to_all x1, blocking collectives, in_one_piece(): lax.all_to_all(both, axis, split_axis=split_dim, concat_axis=concat_dim,...  75.2 us
    unnamed x4, waiting for transfers between devices  58.9 us
    reduce_scatter x1, waiting for transfers between devices, own_block(): parts = lax.psum_scatter(parts, axes[k], scatter_dimension=0, tiled=True)  48 us
    another operation x1, loops' own time, local(): lax.scan(first_pass, 0, (token_blocks, block_expert))  46.4 us
    another operation x1, loops' own time, local(): lax.scan(second_pass, start_acc, (hidden_blocks, source_blocks, weight_bl...  44.4 us
    dot_general x24, matrix products, first_pass(): jnp.dot(block_tokens, up_weight, preferred_element_type=jnp.float32)  44.3 us
  transfers between devices with their start and end apart: 4, of which 4 were waited for; matrix products, arithmetic and copies ran while one was open for 3% of the time, Pallas kernels for 0%

commit v1 on v0

v1 whole, which is shorter than its diff:
```python
import jax
import jax.numpy as jnp
from jax import lax
from jax.experimental import pallas as pl
from jax.experimental.pallas import tpu as pltpu
from jax.sharding import Mesh
from jax.sharding import PartitionSpec as P

MESH = pl.DeviceIdType.MESH
F32, BF16 = jnp.float32, jnp.bfloat16
X, H, Y, L, C = "x", "zh", "y", "zl", "c"
DP = (X, H, Y)
TENSOR = (L, C)
EXPERTS = 4
HALF = 384
ROWS = 80
SHARE = 160


def kernel(
    tok_ref, ids_ref, probs_ref, wg_ref, wu_ref, wd_ref, out_ref,
    wcat, wdown, packed, unpacked, tok_a, tok_b,
    core_out, core_in, lane_out, lane_in, own, hid,
    part_a, part_b, send_a, send_b,
    in1_a, in1_b, in2_a, in2_b, in3,
    sum_a, sum_b, mixed, zsum,
    w_sem, ss, rs,
):
    x, h, y, l, c = (lax.axis_index(a) for a in (X, H, Y, L, C))
    place = {X: x, H: h, Y: y, L: l, C: c}
    pair = 1 - c

    loads = []
    for e in range(EXPERTS):
        loads.append((wg_ref.at[e], wcat.at[:, pl.ds(e * 256, 128)]))
        loads.append((wu_ref.at[e], wcat.at[:, pl.ds(e * 256 + 128, 128)]))
    for e in range(EXPERTS):
        loads.append((wd_ref.at[e], wdown.at[pl.ds(e * 128, 128), :]))
    loads = [pltpu.make_async_copy(s, d, w_sem.at[i]) for i, (s, d) in enumerate(loads)]
    for load in loads:
        load.start()

    def step(axis, by):
        return {axis: lax.rem(place[axis] + by, 4)}

    barrier = pltpu.get_barrier_semaphore()
    partners = [step(a, by) for a in (X, Y, H) for by in (1, 3)]
    partners += [step(L, by) for by in (1, 2, 3)] + [{C: pair}]
    for other in partners:
        pl.semaphore_signal(barrier, inc=1, device_id=other, device_id_type=MESH)
    pl.semaphore_wait(barrier, len(partners))

    sent = []

    def copy(src, dst, i, to):
        return pltpu.make_async_remote_copy(
            src_ref=src, dst_ref=dst, send_sem=ss.at[i], recv_sem=rs.at[i],
            device_id=to, device_id_type=MESH,
        )

    def send(src, dst, i, to):
        one = copy(src, dst, i, to)
        one.start()
        sent.append(one)

    def arrived(dst, i):
        copy(dst, dst, i, {C: pair}).wait_recv()

    class Gather:
        def __init__(self, axis, base, block, half):
            self.axis, self.base, self.block, self.half = axis, base, block, half
            me = place[axis]
            self.me, self.opp = me, lax.rem(me + 2, 4)
            self.right, self.left = lax.rem(me + 1, 4), lax.rem(me + 3, 4)

        def start(self):
            send(self.block(self.me), self.block(self.me), self.base, {self.axis: self.right})
            send(self.block(self.me), self.block(self.me), self.base + 1, {self.axis: self.left})

        def forward(self):
            arrived(self.block(self.left), self.base)
            send(self.half(self.left, 0), self.half(self.left, 0), self.base + 2, {self.axis: self.right})
            arrived(self.block(self.right), self.base + 1)
            send(self.half(self.right, 1), self.half(self.right, 1), self.base + 3, {self.axis: self.left})

        def finish(self):
            arrived(self.half(self.opp, 0), self.base + 2)
            arrived(self.half(self.opp, 1), self.base + 3)

    class Reduce:
        def __init__(self, axis, base, term, out, landing, kind):
            self.axis, self.base, self.term, self.out = axis, base, term, out
            self.landing, self.kind = landing, kind
            me = place[axis]
            self.me, self.opp = me, lax.rem(me + 2, 4)
            self.right, self.left = lax.rem(me + 1, 4), lax.rem(me + 3, 4)

        def start(self):
            to_right, to_left = {self.axis: self.right}, {self.axis: self.left}
            land, b = self.landing, self.base
            send(self.out(self.opp, 0), land(0, 0), b, to_right)
            send(self.out(self.opp, 1), land(0, 1), b + 1, to_left)
            send(self.out(self.right, 1), land(1, 1), b + 2, to_right)
            send(self.out(self.left, 0), land(2, 0), b + 3, to_left)

        def forward(self):
            to_right, to_left = {self.axis: self.right}, {self.axis: self.left}
            land, b = self.landing, self.base
            arrived(land(0, 0), b)
            land(3, 0)[...] = (self.term(self.right, 0)[...] + land(0, 0)[...].astype(F32)).astype(self.kind)
            send(land(3, 0), land(1, 0), b + 4, to_right)
            arrived(land(0, 1), b + 1)
            land(3, 1)[...] = (self.term(self.left, 1)[...] + land(0, 1)[...].astype(F32)).astype(self.kind)
            send(land(3, 1), land(2, 1), b + 5, to_left)

        def finish(self, half):
            land, b = self.landing, self.base
            if half == 0:
                arrived(land(2, 0), b + 3)
                arrived(land(1, 0), b + 4)
            else:
                arrived(land(1, 1), b + 2)
                arrived(land(2, 1), b + 5)
            return self.term(self.me, half)[...] + land(1, half)[...].astype(F32) + land(2, half)[...].astype(F32)

    mine = tok_ref[...].astype(F32)
    tail = [mine[16:20, 256 * j : 256 * (j + 1)] for j in range(3)]
    tail = jnp.concatenate([*tail, jnp.zeros((4, 256), F32)], axis=0)
    packed[h, 0] = mine[0:16, 0:512].astype(BF16)
    packed[h, 1] = jnp.concatenate([mine[0:16, 512:768], tail], axis=1).astype(BF16)
    over_z = Gather(H, 0, lambda i: packed.at[i], lambda i, p: packed.at[i, p])
    over_z.start()
    over_z.forward()
    over_z.finish()
    for i in range(4):
        unpacked[20 * i : 20 * i + 16, 0:512] = packed[i, 0].astype(F32)
        rest = packed[i, 1].astype(F32)
        unpacked[20 * i : 20 * i + 16, 512:768] = rest[:, 0:256]
        for j in range(3):
            unpacked[20 * i + 16 : 20 * i + 20, 256 * j : 256 * (j + 1)] = rest[4 * j : 4 * j + 4, 256:512]
    tok_a[y, x] = unpacked[:, 0:HALF].astype(BF16)
    tok_b[x, y] = unpacked[:, HALF:768].astype(BF16)

    rows_of = ((0, 48), (48, 32))
    first_a = Gather(X, 4, lambda i: tok_a.at[y, i], lambda i, p: tok_a.at[y, i, pl.ds(*rows_of[p]), :])
    first_b = Gather(Y, 8, lambda i: tok_b.at[x, i], lambda i, p: tok_b.at[x, i, pl.ds(*rows_of[p]), :])
    second_a = Gather(Y, 12, lambda i: tok_a.at[i], lambda i, p: tok_a.at[i, pl.ds(2 * p, 2)])
    second_b = Gather(X, 16, lambda i: tok_b.at[i], lambda i, p: tok_b.at[i, pl.ds(2 * p, 2)])
    for a, b in ((first_a, first_b), (second_a, second_b)):
        a.start()
        b.start()
        a.forward()
        b.forward()
        a.finish()
        b.finish()

    for load in loads:
        load.wait()

    def terms(i, core):
        left = jnp.concatenate([tok_a[2 * core, i], tok_a[2 * core + 1, i]], axis=0)
        right = tok_b[i, pl.ds(2 * core, 2)].reshape(SHARE, HALF)
        block = jnp.concatenate([left, right], axis=1)
        ids = ids_ref[i, core]
        picked = [None, None]
        for e in range(EXPERTS):
            both = jnp.dot(block, wcat[:, 256 * e : 256 * (e + 1)], preferred_element_type=F32)
            for k in range(2):
                picked[k] = both if e == 0 else jnp.where(ids[:, k : k + 1] == e, both, picked[k])
        return picked

    def for_pair(d, carry):
        i = lax.rem(l + d, 4)
        for k, value in enumerate(terms(i, pair)):
            core_out[i, :, 256 * k : 256 * (k + 1)] = value
        copy(core_out.at[i], core_in.at[i], 20 + d, {C: pair}).start()
        return carry

    def for_others(d, carry):
        i = lax.rem(l + d, 4)
        picked = terms(i, c)
        arrived(core_in.at[i], 20 + d)
        for k, value in enumerate(picked):
            at = slice(256 * k, 256 * (k + 1))
            lane_out[i, :, at] = (value + core_in[i, :, at]).astype(BF16)
        copy(lane_out.at[i], lane_in.at[d - 1], 24 + d, {L: i}).start()
        return carry

    lax.fori_loop(1, 4, for_pair, 0)
    for k, value in enumerate(terms(l, pair)):
        core_out[l, :, 256 * k : 256 * (k + 1)] = value
    copy(core_out.at[l], core_in.at[l], 20, {C: pair}).start()
    lax.fori_loop(1, 4, for_others, 0)
    picked = terms(l, c)
    arrived(core_in.at[l], 20)
    for k, value in enumerate(picked):
        at = slice(256 * k, 256 * (k + 1))
        own[:, at] = value + core_in[l, :, at]
    for d in (1, 2, 3):
        arrived(lane_in.at[d - 1], 24 + d)

    for k in range(2):
        at = slice(256 * k, 256 * (k + 1))
        total = own[:, at]
        for d in range(3):
            total = total + lane_in[d, :, at].astype(F32)
        gate, up = total[:, :128], total[:, 128:]
        weight = probs_ref[l, c][:, k : k + 1]
        hid[l, c, :, 128 * k : 128 * (k + 1)] = (gate / (1.0 + jnp.exp(-gate)) * up * weight).astype(BF16)

    mine = hid.at[l, c]
    send(mine, mine, 28, {C: pair})
    for d in (1, 2, 3):
        send(mine, mine, 28 + d, step(L, d))

    def second(i, core):
        ids = ids_ref[i, core]
        one, two = hid[i, core, :, 0:128], hid[i, core, :, 128:256]
        one, two = one.astype(F32), two.astype(F32)
        spread = []
        for e in range(EXPERTS):
            here = jnp.where(ids[:, 1:2] == e, two, 0.0)
            spread.append(jnp.where(ids[:, 0:1] == e, one, here).astype(BF16))
        spread = jnp.concatenate(spread, axis=1)
        result = jnp.dot(spread, wdown[...], preferred_element_type=F32)
        for j in range(2):
            piece = result[ROWS * j : ROWS * (j + 1)]
            part_a[i, 2 * core + j] = piece[:, :HALF]
            part_b[2 * core + j, i] = piece[:, HALF:]
            send_a[i, 2 * core + j] = piece[:, :HALF].astype(BF16)
            send_b[2 * core + j, i] = piece[:, HALF:].astype(BF16)

    second(l, c)

    def from_others(d, carry):
        i = lax.rem(l + 4 - d, 4)
        arrived(hid.at[i, c], 28 + d)
        copy(hid.at[i, c], hid.at[i, c], 32 + d, {C: pair}).start()
        second(i, c)
        return carry

    lax.fori_loop(1, 4, from_others, 0)
    arrived(hid.at[l, pair], 28)
    second(l, pair)

    def from_pair(d, carry):
        i = lax.rem(l + 4 - d, 4)
        arrived(hid.at[i, pair], 32 + d)
        second(i, pair)
        return carry

    lax.fori_loop(1, 4, from_pair, 0)

    one_a = Reduce(
        X, 36, lambda i, p: part_a.at[i, pl.ds(2 * p, 2)], lambda i, p: send_a.at[i, pl.ds(2 * p, 2)],
        lambda s, p: in1_a.at[s, pl.ds(2 * p, 2)], BF16,
    )
    one_b = Reduce(
        Y, 42, lambda i, p: part_b.at[i, pl.ds(2 * p, 2)], lambda i, p: send_b.at[i, pl.ds(2 * p, 2)],
        lambda s, p: in1_b.at[s, pl.ds(2 * p, 2)], BF16,
    )
    two_a = Reduce(
        Y, 48, lambda i, p: sum_a.at[i, pl.ds(40 * p, 40)], lambda i, p: sum_a.at[i, pl.ds(40 * p, 40)],
        lambda s, p: in2_a.at[s, pl.ds(40 * p, 40)], F32,
    )
    two_b = Reduce(
        X, 54, lambda i, p: sum_b.at[i, pl.ds(40 * p, 40)], lambda i, p: sum_b.at[i, pl.ds(40 * p, 40)],
        lambda s, p: in2_b.at[s, pl.ds(40 * p, 40)], F32,
    )
    three = Reduce(
        H, 60, lambda i, p: zsum.at[i, p], lambda i, p: zsum.at[i, p], lambda s, p: in3.at[s, p], F32,
    )
    one_a.start()
    one_b.start()
    one_a.forward()
    one_b.forward()
    for half in range(2):
        sum_a[2 * half : 2 * half + 2] = one_a.finish(half)
        sum_b[2 * half : 2 * half + 2] = one_b.finish(half)
    two_a.start()
    two_b.start()
    two_a.forward()
    two_b.forward()
    for half in range(2):
        mixed[40 * half : 40 * half + 40, 0:HALF] = two_a.finish(half)
        mixed[40 * half : 40 * half + 40, HALF:768] = two_b.finish(half)
    zsum[...] = jnp.zeros_like(zsum)
    for i in range(4):
        for p in range(2):
            zsum[i, p, 0:20] = mixed[20 * i : 20 * i + 20, HALF * p : HALF * (p + 1)]
    three.start()
    three.forward()
    for p in range(2):
        out_ref[:, HALF * p : HALF * (p + 1)] = three.finish(p)[0:20].astype(BF16)

    for one in sent:
        one.wait_send()

    def drain(d, carry):
        i = lax.rem(l + d, 4)
        copy(core_out.at[i], core_in.at[i], 20 + d, {C: pair}).wait_send()
        copy(lane_out.at[i], lane_in.at[d - 1], 24 + d, {L: i}).wait_send()
        back = lax.rem(l + 4 - d, 4)
        copy(hid.at[back, c], hid.at[back, c], 32 + d, {C: pair}).wait_send()
        return carry

    lax.fori_loop(1, 4, drain, 0)
    copy(core_out.at[l], core_in.at[l], 20, {C: pair}).wait_send()


def local(tokens, route_ids, route_probs, w_gate, w_up, w_down):
    def arranged(a):
        a = a.reshape(4, 4, 4, 20, 2).transpose(0, 2, 1, 3, 4)
        return a.reshape(4, 2, SHARE, 2)

    ids = arranged(route_ids)
    probs = arranged(route_probs.astype(F32))
    vmem = pl.BlockSpec(memory_space=pltpu.VMEM)
    hbm = pl.BlockSpec(memory_space=pl.ANY)
    return pl.pallas_call(
        kernel,
        out_shape=jax.ShapeDtypeStruct((20, 768), BF16),
        in_specs=[vmem, vmem, vmem, hbm, hbm, hbm],
        out_specs=vmem,
        scratch_shapes=[
            pltpu.VMEM((768, 1024), BF16),
            pltpu.VMEM((512, 768), BF16),
            pltpu.VMEM((4, 2, 16, 512), BF16),
            pltpu.VMEM((ROWS, 768), F32),
            pltpu.VMEM((4, 4, ROWS, HALF), BF16),
            pltpu.VMEM((4, 4, ROWS, HALF), BF16),
            pltpu.VMEM((4, SHARE, 512), F32),
            pltpu.VMEM((4, SHARE, 512), F32),
            pltpu.VMEM((4, SHARE, 512), BF16),
            pltpu.VMEM((3, SHARE, 512), BF16),
            pltpu.VMEM((SHARE, 512), F32),
            pltpu.VMEM((4, 2, SHARE, 256), BF16),
            pltpu.VMEM((4, 4, ROWS, HALF), F32),
            pltpu.VMEM((4, 4, ROWS, HALF), F32),
            pltpu.VMEM((4, 4, ROWS, HALF), BF16),
            pltpu.VMEM((4, 4, ROWS, HALF), BF16),
            pltpu.VMEM((4, 4, ROWS, HALF), BF16),
            pltpu.VMEM((4, 4, ROWS, HALF), BF16),
            pltpu.VMEM((4, ROWS, HALF), F32),
            pltpu.VMEM((4, ROWS, HALF), F32),
            pltpu.VMEM((4, 2, 24, HALF), F32),
            pltpu.VMEM((4, ROWS, HALF), F32),
            pltpu.VMEM((4, ROWS, HALF), F32),
            pltpu.VMEM((ROWS, 768), F32),
            pltpu.VMEM((4, 2, 24, HALF), F32),
            pltpu.SemaphoreType.DMA((12,)),
            pltpu.SemaphoreType.DMA((66,)),
            pltpu.SemaphoreType.DMA((66,)),
        ],
        compiler_params=pltpu.CompilerParams(
            collective_id=0, has_side_effects=True, vmem_limit_bytes=40 * 2**20
        ),
    )(tokens, ids, probs, w_gate, w_up, w_down)


def solution(mesh):
    torus = Mesh(mesh.devices.reshape(4, 4, 4, 4, 2), (X, H, Y, L, C))
    in_specs = (
        P(DP, TENSOR),
        P(),
        P(),
        P(None, TENSOR, DP),
        P(None, TENSOR, DP),
        P(None, DP, TENSOR),
    )
    return jax.shard_map(local, mesh=torus, in_specs=in_specs, out_specs=P(DP, TENSOR), check_vma=False)
```

time: 810 us -> 110 us (0.14)
  the two profiles are of different devices: /device:TPU:1 before, /device:TPU:16 now
where the time goes in v1:
time: 110 us
  Pallas kernels  105 us (95%)
  local copies, waits for them, and re-layouts  4.69 us (4%)
    pallas_call x1, Pallas kernels, local(): pl.pallas_call(kernel, out_shape=jax.ShapeDtypeStruct((20, 768), BF16), i...  105 us
    unnamed x11, local copies, waits for them, and re-layouts  2.9 us

profile of v1, /device:TPU:16, one launch (start us, length us, event | category | flops | bytes accessed | tf_op | source)
XLA Modules:
  0.0 109.9 jit_solution(9789220965752861302)
XLA Ops:
  0.0 0.8 reshape.15
  0.9 0.0 copy-start.4
  0.9 0.1 reshape.16
  1.0 0.6 copy-done.4
  1.6 0.0 copy-start.1
  1.6 0.1 reshape.24
  1.7 0.0 copy-start
  1.7 0.1 reshape.21
  1.8 0.3 copy.12.probs_ref
  2.1 0.0 copy-start.3
  2.2 0.3 copy.11.ids_ref
  2.4 0.2 copy-done.1
  2.7 0.3 copy-done
  3.0 0.1 copy-done.3
  3.0 0.0 copy-start.2
  3.0 1.1 %copy-done.2 = bf16[4,128,768]{2,1,0:T(8,128)(2,1)S(1)} copy-done((bf16[4,128,768]{2,1,0:T(8,128)(2,1)S(1)}, bf16[4,128,768]{2,1,0:T(8,128)(2,1)}, u32[]{:S(2)}) %copy-start.2) | copy-done | bytes 786456
  4.2 105.1 %shard_map.64 = bf16[20,768]{1,0:T(8,128)(2,1)S(1)} custom-call(bf16[20,768]{1,0:T(8,128)(2,1)S(1)} %copy-done.3, s32[4,2,160,2]{3,2,1,0:T(8,128)S(1)} %copy.11.ids_ref, f32[4,2,160,2]{3,2,1,0:T(8,128)S(1)} %copy.12.probs_ref, bf16[4,768,128]{2,1,0:T(8,128)(2,1)S(1)} %copy-done, bf16[4,768,128]{2,1,0:T(8,128)(2,1)S(1)} %copy-done.1, ...), custom_call_target="tpu_custom_call" | custom-call | tf_op jit(solution)/shard_map/pallas_call | solution.py:320
  109.3 0.6 copy.18
  (2 shorter events, 0.0 us)
Async XLA Ops:
  0.9 0.7 copy-start.4
  1.6 1.1 %copy-start.1 = (bf16[4,768,128]{2,1,0:T(8,128)(2,1)S(1)}, bf16[4,768,128]{2,1,0:T(8,128)(2,1)}, u32[]{:S(2)}) copy-start(bf16[4,768,128]{2,1,0:T(8,128)(2,1)} %wu_ref.1) | copy-start | bytes 2359300
  1.7 1.3 %copy-start = (bf16[4,768,128]{2,1,0:T(8,128)(2,1)S(1)}, bf16[4,768,128]{2,1,0:T(8,128)(2,1)}, u32[]{:S(2)}) copy-start(bf16[4,768,128]{2,1,0:T(8,128)(2,1)} %wg_ref.1) | copy-start | bytes 2359300
  2.1 0.9 copy-start.3
  3.0 1.1 %copy-start.2 = (bf16[4,128,768]{2,1,0:T(8,128)(2,1)S(1)}, bf16[4,128,768]{2,1,0:T(8,128)(2,1)}, u32[]{:S(2)}) copy-start(bf16[4,128,768]{2,1,0:T(8,128)(2,1)} %wd_ref.1) | copy-start | bytes 2359300

commit v2 on v0

v2 whole, which is shorter than its diff:
```python
import jax
import jax.numpy as jnp
from jax import lax
from jax.experimental import pallas as pl
from jax.experimental.pallas import tpu as pltpu
from jax.sharding import Mesh
from jax.sharding import PartitionSpec as P

MESH = pl.DeviceIdType.MESH
F32, BF16 = jnp.float32, jnp.bfloat16
X, H, Y, L, C = "x", "zh", "y", "zl", "c"
DP = (X, H, Y)
TENSOR = (L, C)
EXPERTS = 4
WIDTH = 768
PIECE = 40
GROUP = 160


def kernel(
    tok_hbm, ids_hbm, probs_hbm, wg_ref, wu_ref, wd_ref, out_ref,
    tok_in, ids_in, probs_in, wcat, wdown, meta, packed, unpacked, tok,
    core_out, core_in, own, lane_out, lane_in, hid,
    part, send_part, in1, total, in2, z_own, z_out, z_in,
    w_sem, ss, rs,
):
    x, h, y, l, c = (lax.axis_index(a) for a in (X, H, Y, L, C))
    place = {X: x, H: h, Y: y, L: l, C: c}
    pair = 1 - c

    small = [(tok_hbm, tok_in), (ids_hbm, ids_in), (probs_hbm, probs_in)]
    loads = []
    for e in range(EXPERTS):
        loads.append((wg_ref.at[e], wcat.at[:, pl.ds(e * 256, 128)]))
        loads.append((wu_ref.at[e], wcat.at[:, pl.ds(e * 256 + 128, 128)]))
    for e in range(EXPERTS):
        loads.append((wd_ref.at[e], wdown.at[pl.ds(e * 128, 128), :]))
    loads = [pltpu.make_async_copy(s, d, w_sem.at[i]) for i, (s, d) in enumerate(small + loads)]
    for load in loads:
        load.start()

    def step(axis, by):
        return {axis: lax.rem(place[axis] + by, 4)}

    barrier = pltpu.get_barrier_semaphore()
    partners = [step(a, by) for a in (X, Y, H, L) for by in (1, 2, 3)] + [{C: pair}]
    for other in partners:
        pl.semaphore_signal(barrier, inc=1, device_id=other, device_id_type=MESH)

    sent, numbers = [], {}

    def copy(src, dst, key, to):
        i = numbers.setdefault(key, len(numbers))
        return pltpu.make_async_remote_copy(
            src_ref=src, dst_ref=dst, send_sem=ss.at[i], recv_sem=rs.at[i],
            device_id=to, device_id_type=MESH,
        )

    def send(src, dst, key, to):
        one = copy(src, dst, key, to)
        one.start()
        sent.append(one)

    def arrived(dst, key):
        copy(dst, dst, key, {C: pair}).wait_recv()

    def outer_place(r):
        return y + r * (x - y)

    def inner_place(r):
        return x + r * (y - x)

    def outer_to(r, o):
        return {X: x + r * (o - x), Y: o + r * (y - o)}

    def inner_to(r, i):
        return {X: i + r * (x - i), Y: y + r * (i - y)}

    def at(place_, d):
        return lax.rem(place_ + d, 4)

    for load in loads[:3]:
        load.wait()
    row = lax.broadcasted_iota(jnp.int32, (640, 1), 0)

    def count(value, size, most):
        return sum((value >= size * k).astype(jnp.int32) for k in range(1, most))

    xb = count(row, 320, 2)
    rest = row - 320 * xb
    part_of = count(rest, 160, 2)
    rest = rest - 160 * part_of
    yy = count(rest, PIECE, 4)
    rest = rest - PIECE * yy
    zz = count(rest, 20, 2)
    source = 320 * xb + (2 * part_of + zz) * 80 + yy * 20 + rest - 20 * zz
    order = (lax.broadcasted_iota(jnp.int32, (640, 640), 1) == source).astype(F32).astype(BF16)
    lines = jnp.concatenate([ids_in[...].astype(F32), probs_in[...].astype(F32), jnp.zeros((4, 1280), F32)], axis=0)
    lines = lines.astype(BF16)
    for two in range(2):
        columns = lax.dot_general(
            order, lines[:, 640 * two : 640 * (two + 1)], (((1,), (1,)), ((), ())), preferred_element_type=F32
        )
        for one in range(2):
            for yi in range(4):
                xi = 2 * two + one
                at0 = 320 * one + PIECE * yi
                meta[0, yi, xi] = columns[at0 : at0 + PIECE]
                meta[1, xi, yi] = columns[at0 + 160 : at0 + 160 + PIECE]

    def pack(block):
        tail = [block[16:20, 256 * j : 256 * (j + 1)] for j in range(3)]
        tail = jnp.concatenate([*tail, jnp.zeros((4, 256), F32)], axis=0)
        return jnp.concatenate([block[0:16], tail], axis=1).astype(BF16)

    packed[h] = pack(tok_in[...].astype(F32))
    pl.semaphore_wait(barrier, len(partners))

    for d in (1, 2, 3):
        send(packed.at[h], packed.at[h], ("z", d), step(H, d))
    for d in (1, 3, 2):
        arrived(packed.at[at(h, 4 - d)], ("z", d))
    for i in range(4):
        block = packed[i].astype(F32)
        unpacked[20 * i : 20 * i + 16] = block[:, 0:WIDTH]
        for j in range(3):
            unpacked[20 * i + 16 : 20 * i + 20, 256 * j : 256 * (j + 1)] = block[4 * j : 4 * j + 4, WIDTH:]
    for r in range(2):
        mine = tok.at[r, outer_place(r), inner_place(r)]
        mine[...] = unpacked[PIECE * r : PIECE * (r + 1)].astype(BF16)
        for d in (1, 3, 2):
            send(mine, mine, ("t", r, d), inner_to(r, at(inner_place(r), d)))
    for r in range(2):
        for d in (1, 3, 2):
            arrived(tok.at[r, outer_place(r), at(inner_place(r), 4 - d)], ("t", r, d))
        mine = tok.at[r, outer_place(r)]
        for d in (1, 3, 2):
            send(mine, mine, ("T", r, d), outer_to(r, at(outer_place(r), d)))
    for load in loads[3:]:
        load.wait()

    def terms(r, d):
        o = at(outer_place(r), d)
        block = tok[r, o].astype(F32).reshape(GROUP, WIDTH).astype(BF16)
        ids = meta[r, o].reshape(GROUP, 8)
        picked = [None, None]
        for e in range(EXPERTS):
            both = jnp.dot(block, wcat[:, 256 * e : 256 * (e + 1)], preferred_element_type=F32)
            for k in range(2):
                picked[k] = both if e == 0 else jnp.where(ids[:, k : k + 1] == float(e), both, picked[k])
        return picked

    def for_pair(d):
        for k, value in enumerate(terms(pair, d)):
            core_out[d, :, 256 * k : 256 * (k + 1)] = value
        send(core_out.at[d], core_in.at[d], ("c", d), {C: pair})

    def for_lanes(d):
        picked = terms(c, d)
        arrived(core_in.at[d], ("c", d))
        for k, value in enumerate(picked):
            cols = slice(256 * k, 256 * (k + 1))
            value = (value + core_in[d, :, cols]).reshape(4, PIECE, 256)
            own[d, :, :, cols] = value
            lane_out[d, :, :, cols] = value.astype(BF16)
        for j in (2, 3, 1):
            i = at(l, j)
            send(lane_out.at[d, i], lane_in.at[d, j - 1], ("l", d, j), {L: i})

    def hidden(d):
        o = at(outer_place(c), d)
        for j in (1, 3, 2):
            arrived(lane_in.at[d, j - 1], ("l", d, j))
        for k in range(2):
            cols = slice(256 * k, 256 * (k + 1))
            sums = own[d, l, :, cols]
            for j in range(3):
                sums = sums + lane_in[d, j, :, cols].astype(F32)
            gate, up = sums[:, :128], sums[:, 128:]
            weight = meta[c, o, l][:, 2 + k : 3 + k]
            hid[c, o, l, :, 128 * k : 128 * (k + 1)] = (gate / (1.0 + jnp.exp(-gate)) * up * weight).astype(BF16)
        mine = hid.at[c, o, l]
        for j in (2, 3, 1):
            send(mine, mine, ("h", d, j), step(L, j))
        send(mine, mine, ("p", d, 0), {C: pair})

    def forward(d):
        o = at(outer_place(c), d)
        for j in (1, 3, 2):
            piece = hid.at[c, o, at(l, 4 - j)]
            arrived(piece, ("h", d, j))
            send(piece, piece, ("p", d, j), {C: pair})

    def second(r, d, name):
        o = at(outer_place(r), d)
        if name == "pair":
            for j in range(4):
                arrived(hid.at[r, o, at(l, 4 - j)], ("p", d, j))
        ids = meta[r, o].reshape(GROUP, 8)
        units = hid[r, o].astype(F32).reshape(GROUP, 256)
        one, two = units[:, 0:128], units[:, 128:256]
        spread = []
        for e in range(EXPERTS):
            here = jnp.where(ids[:, 1:2] == float(e), two, 0.0)
            spread.append(jnp.where(ids[:, 0:1] == float(e), one, here).astype(BF16))
        spread = jnp.concatenate(spread, axis=1)
        result = jnp.dot(spread, wdown[...], preferred_element_type=F32).reshape(4, PIECE, WIDTH)
        if d == 0:
            part[r] = result
        else:
            send_part[r, d - 1] = result.astype(BF16)
            send(send_part.at[r, d - 1], in1.at[r, d - 1], ("s", name, d), outer_to(r, o))

    for_pair(0)
    for_lanes(0)
    for d in (1, 3, 2):
        for r in range(2):
            arrived(tok.at[r, at(outer_place(r), d)], ("T", r, 4 - d))
        for_pair(d)
        for_lanes(d)
        if d == 3:
            hidden(0)
    hidden(1)
    forward(0)
    hidden(3)
    forward(1)
    second(c, 1, "own")
    hidden(2)
    forward(3)
    second(pair, 1, "pair")
    second(c, 3, "own")
    second(pair, 3, "pair")
    forward(2)
    second(c, 2, "own")
    second(pair, 2, "pair")
    second(c, 0, "own")
    second(pair, 0, "pair")

    for name, r in (("own", c), ("pair", pair)):
        for d in (1, 3, 2):
            arrived(in1.at[r, d - 1], ("s", name, d))
        value = part[r]
        for d in range(3):
            value = value + in1[r, d].astype(F32)
        total[r] = value
        for d in (1, 3, 2):
            i = at(inner_place(r), d)
            send(total.at[r, i], in2.at[r, d - 1], ("S", name, d), inner_to(r, i))
    for name, r in (("own", c), ("pair", pair)):
        for d in (1, 3, 2):
            arrived(in2.at[r, d - 1], ("S", name, d))
    for r in range(2):
        value = total[r, inner_place(r)]
        for d in range(3):
            value = value + in2[r, d]
        for zi in range(2):
            block = value[20 * zi : 20 * (zi + 1)]
            z_own[2 * r + zi] = block
            z_out[2 * r + zi] = pack(block)
    for d in (2, 1, 3):
        i = at(h, d)
        send(z_out.at[i], z_in.at[d - 1], ("Z", d), {H: i})
    for d in (1, 3, 2):
        arrived(z_in.at[d - 1], ("Z", d))
    value = z_in[0].astype(F32) + z_in[1].astype(F32) + z_in[2].astype(F32)
    mine = z_own[h]
    bottom = jnp.concatenate([value[4 * j : 4 * j + 4, WIDTH:] for j in range(3)], axis=1)
    out_ref[...] = (mine + jnp.concatenate([value[:, :WIDTH], bottom], axis=0)).astype(BF16)

    for one in sent:
        one.wait_send()


def local(tokens, route_ids, route_probs, w_gate, w_up, w_down):
    hbm = pl.BlockSpec(memory_space=pl.ANY)
    return pl.pallas_call(
        kernel,
        out_shape=jax.ShapeDtypeStruct((20, WIDTH), BF16),
        in_specs=[hbm] * 6,
        out_specs=pl.BlockSpec(memory_space=pltpu.VMEM),
        scratch_shapes=[
            pltpu.VMEM((20, WIDTH), BF16),
            pltpu.VMEM((2, 1280), jnp.int32),
            pltpu.VMEM((2, 1280), BF16),
            pltpu.VMEM((WIDTH, 1024), BF16),
            pltpu.VMEM((512, WIDTH), BF16),
            pltpu.VMEM((2, 4, 4, PIECE, 8), F32),
            pltpu.VMEM((4, 16, 1024), BF16),
            pltpu.VMEM((80, WIDTH), F32),
            pltpu.VMEM((2, 4, 4, PIECE, WIDTH), BF16),
            pltpu.VMEM((4, GROUP, 512), F32),
            pltpu.VMEM((4, GROUP, 512), F32),
            pltpu.VMEM((4, 4, PIECE, 512), F32),
            pltpu.VMEM((4, 4, PIECE, 512), BF16),
            pltpu.VMEM((4, 3, PIECE, 512), BF16),
            pltpu.VMEM((2, 4, 4, PIECE, 256), BF16),
            pltpu.VMEM((2, 4, PIECE, WIDTH), F32),
            pltpu.VMEM((2, 3, 4, PIECE, WIDTH), BF16),
            pltpu.VMEM((2, 3, 4, PIECE, WIDTH), BF16),
            pltpu.VMEM((2, 4, PIECE, WIDTH), F32),
            pltpu.VMEM((2, 3, PIECE, WIDTH), F32),
            pltpu.VMEM((4, 20, WIDTH), F32),
            pltpu.VMEM((4, 16, 1024), BF16),
            pltpu.VMEM((3, 16, 1024), BF16),
            pltpu.SemaphoreType.DMA((15,)),
            pltpu.SemaphoreType.DMA((80,)),
            pltpu.SemaphoreType.DMA((80,)),
        ],
        compiler_params=pltpu.CompilerParams(
            collective_id=0, has_side_effects=True, vmem_limit_bytes=60 * 2**20
        ),
    )(tokens, route_ids.T, route_probs.T, w_gate, w_up, w_down)


def solution(mesh):
    torus = Mesh(mesh.devices.reshape(4, 4, 4, 4, 2), (X, H, Y, L, C))
    in_specs = (
        P(DP, TENSOR),
        P(),
        P(),
        P(None, TENSOR, DP),
        P(None, TENSOR, DP),
        P(None, DP, TENSOR),
    )
    return jax.shard_map(local, mesh=torus, in_specs=in_specs, out_specs=P(DP, TENSOR), check_vma=False)
```

time: 810 us -> 95 us (0.12); the launches traced: 802 us -> 94.8 us
  waiting for transfers between devices: 227 us -> 0 us
  other arithmetic: 153 us -> 0 us
  blocking collectives: 110 us -> 0 us
  local copies, waits for them, and re-layouts: 102 us -> 1.39 us
  matrix products: 100 us -> 0 us
  Pallas kernels: 0 us -> 93.4 us
  loops' own time: 90.8 us -> 0 us
  between operations: 13.9 us -> 0.01 us
    scatter-add x24 -> x0, other arithmetic: 129 us -> none  [second_pass(): mixed_acc.at[block_source].add(out_block * block_weight[:, None])]
    all_gather x1 -> x0, waiting for transfers between devices: 111 us -> none  [local(): all_tokens = lax.all_gather(tokens, DP, axis=0, tiled=True)]
    dot_general x72 -> x0, matrix products: 100 us -> none  [the longest x24 44.3 us: first_pass(): jnp.dot(block_tokens, up_weight, preferred_element_type=jnp.float32)]
    pallas_call x0 -> x1, Pallas kernels: none -> 93.4 us  [local(): pl.pallas_call(kernel, out_shape=jax.ShapeDtypeStruct((20, WIDTH), BF16),...]
    another operation x2 -> x0, loops' own time: 90.8 us -> none  [the longest x1 46.4 us: local(): lax.scan(first_pass, 0, (token_blocks, block_expert))]
    all_to_all x1 -> x0, blocking collectives: 75.2 us -> none  [in_one_piece(): lax.all_to_all(both, axis, split_axis=split_dim, concat_axis=concat_dim,...]
    unnamed x4 -> x0, waiting for transfers between devices: 58.9 us -> none
    reduce_scatter x1 -> x0, waiting for transfers between devices: 48 us -> none  [own_block(): parts = lax.psum_scatter(parts, axes[k], scatter_dimension=0, tiled=True)]
  transfers between devices with their start and end apart: 4 -> 0, of which waited for: 4 -> 0; matrix products, arithmetic and copies ran while one was open for 3% -> 0% of each run, Pallas kernels for 0% -> 0%
where the time goes in v2:
time: 95 us; the launch traced here: 94.8 us
  Pallas kernels  93.4 us (98%)
  local copies, waits for them, and re-layouts  1.39 us (1%)
    pallas_call x1, Pallas kernels, local(): pl.pallas_call(kernel, out_shape=jax.ShapeDtypeStruct((20, WIDTH), BF16),...  93.4 us

profile of v2, /device:TPU:1, one launch (start us, length us, event | category | flops | bytes accessed | tf_op | source)
XLA Modules:
  0.0 94.8 jit_solution(7806699079536702760)
XLA Ops:
  0.0 93.4 %shard_map.64 = bf16[20,768]{1,0:T(8,128)(2,1)} custom-call(bf16[20,768]{1,0:T(8,128)(2,1)} %tok_hbm.1, s32[2,1280]{1,0:T(2,128)} %bitcast.2, bf16[2,1280]{1,0:T(2,128)(2,1)} %bitcast.3, bf16[4,768,128]{2,1,0:T(8,128)(2,1)} %wg_ref.1, bf16[4,768,128]{2,1,0:T(8,128)(2,1)} %wu_ref.1, bf16[4,128,768]{2,1,0:T(8,128)(2,1)} %wd_ref.1), custom_call_target="tpu_custom_call" | custom-call | tf_op jit(solution)/shard_map/pallas_call | solution.py:276
  93.4 1.4 %copy.8 = bf16[20,768]{1,0:T(8,128)(2,1)} copy(bf16[20,768]{1,0:T(8,128)(2,1)} %shard_map.64) | data formatting | bytes 61440

commit v3 on v2

--- a/solution.py
+++ b/solution.py
@@ -21,7 +21,7 @@
     tok_hbm, ids_hbm, probs_hbm, wg_ref, wu_ref, wd_ref, out_ref,
     tok_in, ids_in, probs_in, wcat, wdown, meta, packed, unpacked, tok,
     core_out, core_in, own, lane_out, lane_in, hid,
-    part, send_part, in1, total, in2, z_own, z_out, z_in,
+    part, send_part, in1, total, send_total, in2, z_own, z_out, z_in,
     w_sem, ss, rs,
 ):
     x, h, y, l, c = (lax.axis_index(a) for a in (X, H, Y, L, C))
@@ -81,6 +81,16 @@
 
     for load in loads[:3]:
         load.wait()
+    def pack(block):
+        tail = [block[16:20, 256 * j : 256 * (j + 1)] for j in range(3)]
+        tail = jnp.concatenate([*tail, jnp.zeros((4, 256), F32)], axis=0)
+        return jnp.concatenate([block[0:16], tail], axis=1).astype(BF16)
+
+    packed[h] = pack(tok_in[...].astype(F32))
+    pl.semaphore_wait(barrier, len(partners))
+
+    for d in (1, 2, 3):
+        send(packed.at[h], packed.at[h], ("z", d), step(H, d))
     row = lax.broadcasted_iota(jnp.int32, (640, 1), 0)
 
     def count(value, size, most):
@@ -108,16 +118,6 @@
                 meta[0, yi, xi] = columns[at0 : at0 + PIECE]
                 meta[1, xi, yi] = columns[at0 + 160 : at0 + 160 + PIECE]
 
-    def pack(block):
-        tail = [block[16:20, 256 * j : 256 * (j + 1)] for j in range(3)]
-        tail = jnp.concatenate([*tail, jnp.zeros((4, 256), F32)], axis=0)
-        return jnp.concatenate([block[0:16], tail], axis=1).astype(BF16)
-
-    packed[h] = pack(tok_in[...].astype(F32))
-    pl.semaphore_wait(barrier, len(partners))
-
-    for d in (1, 2, 3):
-        send(packed.at[h], packed.at[h], ("z", d), step(H, d))
     for d in (1, 3, 2):
         arrived(packed.at[at(h, 4 - d)], ("z", d))
     for i in range(4):
@@ -125,17 +125,36 @@
         unpacked[20 * i : 20 * i + 16] = block[:, 0:WIDTH]
         for j in range(3):
             unpacked[20 * i + 16 : 20 * i + 20, 256 * j : 256 * (j + 1)] = block[4 * j : 4 * j + 4, WIDTH:]
+    def share_block(r, d, k):
+        mine = tok.at[r, outer_place(r), at(inner_place(r), k)]
+        send(mine, mine, ("T", r, d, k), outer_to(r, at(outer_place(r), d)))
+
+    def share_group(r, d):
+        mine = tok.at[r, outer_place(r)]
+        send(mine, mine, ("T", r, d), outer_to(r, at(outer_place(r), d)))
+
+    def group_arrived(d):
+        for r in range(2):
+            o = at(outer_place(r), d)
+            if d == 2:
+                arrived(tok.at[r, o], ("T", r, d))
+            else:
+                for k in (0, 3, 1, 2):
+                    arrived(tok.at[r, o, at(inner_place(r), k)], ("T", r, 4 - d, k))
+
     for r in range(2):
         mine = tok.at[r, outer_place(r), inner_place(r)]
         mine[...] = unpacked[PIECE * r : PIECE * (r + 1)].astype(BF16)
         for d in (1, 3, 2):
             send(mine, mine, ("t", r, d), inner_to(r, at(inner_place(r), d)))
     for r in range(2):
-        for d in (1, 3, 2):
+        share_block(r, 1, 0)
+        share_block(r, 3, 0)
+    for d in (1, 3, 2):
+        for r in range(2):
             arrived(tok.at[r, outer_place(r), at(inner_place(r), 4 - d)], ("t", r, d))
-        mine = tok.at[r, outer_place(r)]
-        for d in (1, 3, 2):
-            send(mine, mine, ("T", r, d), outer_to(r, at(outer_place(r), d)))
+            share_block(r, 1, 4 - d)
+            share_block(r, 3, 4 - d)
     for load in loads[3:]:
         load.wait()
 
@@ -213,26 +232,31 @@
 
     for_pair(0)
     for_lanes(0)
-    for d in (1, 3, 2):
-        for r in range(2):
-            arrived(tok.at[r, at(outer_place(r), d)], ("T", r, 4 - d))
-        for_pair(d)
-        for_lanes(d)
-        if d == 3:
-            hidden(0)
+    group_arrived(1)
+    group_arrived(3)
+    share_group(0, 2)
+    share_group(1, 2)
+    for_pair(1)
+    for_pair(3)
+    for_lanes(1)
+    for_lanes(3)
+    group_arrived(2)
+    for_pair(2)
+    for_lanes(2)
     hidden(1)
-    forward(0)
     hidden(3)
     forward(1)
     second(c, 1, "own")
-    hidden(2)
     forward(3)
     second(pair, 1, "pair")
     second(c, 3, "own")
     second(pair, 3, "pair")
+    hidden(2)
+    hidden(0)
     forward(2)
     second(c, 2, "own")
     second(pair, 2, "pair")
+    forward(0)
     second(c, 0, "own")
     second(pair, 0, "pair")
 
@@ -243,21 +267,22 @@
         for d in range(3):
             value = value + in1[r, d].astype(F32)
         total[r] = value
+        send_total[r] = value.astype(BF16)
         for d in (1, 3, 2):
             i = at(inner_place(r), d)
-            send(total.at[r, i], in2.at[r, d - 1], ("S", name, d), inner_to(r, i))
+            send(send_total.at[r, i], in2.at[r, d - 1], ("S", name, d), inner_to(r, i))
     for name, r in (("own", c), ("pair", pair)):
         for d in (1, 3, 2):
             arrived(in2.at[r, d - 1], ("S", name, d))
     for r in range(2):
         value = total[r, inner_place(r)]
         for d in range(3):
-            value = value + in2[r, d]
+            value = value + in2[r, d].astype(F32)
         for zi in range(2):
             block = value[20 * zi : 20 * (zi + 1)]
             z_own[2 * r + zi] = block
             z_out[2 * r + zi] = pack(block)
-    for d in (2, 1, 3):
+    for d in (1, 3, 2):
         i = at(h, d)
         send(z_out.at[i], z_in.at[d - 1], ("Z", d), {H: i})
     for d in (1, 3, 2):
@@ -298,13 +323,14 @@
             pltpu.VMEM((2, 3, 4, PIECE, WIDTH), BF16),
             pltpu.VMEM((2, 3, 4, PIECE, WIDTH), BF16),
             pltpu.VMEM((2, 4, PIECE, WIDTH), F32),
-            pltpu.VMEM((2, 3, PIECE, WIDTH), F32),
+            pltpu.VMEM((2, 4, PIECE, WIDTH), BF16),
+            pltpu.VMEM((2, 3, PIECE, WIDTH), BF16),
             pltpu.VMEM((4, 20, WIDTH), F32),
             pltpu.VMEM((4, 16, 1024), BF16),
             pltpu.VMEM((3, 16, 1024), BF16),
             pltpu.SemaphoreType.DMA((15,)),
-            pltpu.SemaphoreType.DMA((80,)),
-            pltpu.SemaphoreType.DMA((80,)),
+            pltpu.SemaphoreType.DMA((96,)),
+            pltpu.SemaphoreType.DMA((96,)),
         ],
         compiler_params=pltpu.CompilerParams(
             collective_id=0, has_side_effects=True, vmem_limit_bytes=60 * 2**20

time: 95 us -> 89.6 us (0.943)
  Pallas kernels: 93.4 us -> 88 us
    pallas_call x1, Pallas kernels: 93.4 us -> 88 us  [local(): pl.pallas_call(kernel, out_shape=jax.ShapeDtypeStruct((20, WIDTH), BF16),...]
where the time goes in v3:
time: 89.6 us; the launch traced here: 89.4 us
  Pallas kernels  88 us (98%)
  local copies, waits for them, and re-layouts  1.39 us (2%)
    pallas_call x1, Pallas kernels, local(): pl.pallas_call(kernel, out_shape=jax.ShapeDtypeStruct((20, WIDTH), BF16),...  88 us

profile of v3, /device:TPU:1, one launch (start us, length us, event | category | flops | bytes accessed | tf_op | source)
XLA Modules:
  0.0 89.4 jit_solution(12410711801603771023)
XLA Ops:
  0.0 88.0 %shard_map.64 = bf16[20,768]{1,0:T(8,128)(2,1)} custom-call(bf16[20,768]{1,0:T(8,128)(2,1)} %tok_hbm.1, s32[2,1280]{1,0:T(2,128)} %bitcast.2, bf16[2,1280]{1,0:T(2,128)(2,1)} %bitcast.3, bf16[4,768,128]{2,1,0:T(8,128)(2,1)} %wg_ref.1, bf16[4,768,128]{2,1,0:T(8,128)(2,1)} %wu_ref.1, bf16[4,128,768]{2,1,0:T(8,128)(2,1)} %wd_ref.1), custom_call_target="tpu_custom_call" | custom-call | tf_op jit(solution)/shard_map/pallas_call | solution.py:301
  88.0 1.4 %copy.8 = bf16[20,768]{1,0:T(8,128)(2,1)} copy(bf16[20,768]{1,0:T(8,128)(2,1)} %shard_map.64) | data formatting | bytes 61440

commit v4 on v3

--- a/solution.py
+++ b/solution.py
@@ -49,8 +49,11 @@
 
     sent, numbers = [], {}
 
+    def number(key):
+        return numbers.setdefault(key, len(numbers))
+
     def copy(src, dst, key, to):
-        i = numbers.setdefault(key, len(numbers))
+        i = number(key) if isinstance(key, tuple) else key
         return pltpu.make_async_remote_copy(
             src_ref=src, dst_ref=dst, send_sem=ss.at[i], recv_sem=rs.at[i],
             device_id=to, device_id_type=MESH,
@@ -129,18 +132,18 @@
         mine = tok.at[r, outer_place(r), at(inner_place(r), k)]
         send(mine, mine, ("T", r, d, k), outer_to(r, at(outer_place(r), d)))
 
-    def share_group(r, d):
-        mine = tok.at[r, outer_place(r)]
-        send(mine, mine, ("T", r, d), outer_to(r, at(outer_place(r), d)))
-
-    def group_arrived(d):
+    def pass_on(k):
         for r in range(2):
-            o = at(outer_place(r), d)
-            if d == 2:
-                arrived(tok.at[r, o], ("T", r, d))
-            else:
-                for k in (0, 3, 1, 2):
-                    arrived(tok.at[r, o, at(inner_place(r), k)], ("T", r, 4 - d, k))
+            for d, blocks in ((3, (0, 1)), (1, (3, 2))):
+                block = tok.at[r, at(outer_place(r), d), at(inner_place(r), k)]
+                arrived(block, ("T", r, 4 - d, k))
+                if k in blocks:
+                    send(block, block, ("T", r, 2, k), outer_to(r, at(outer_place(r), 4 - d)))
+
+    def opposite_arrived():
+        for r in range(2):
+            for k in range(4):
+                arrived(tok.at[r, at(outer_place(r), 2), at(inner_place(r), k)], ("T", r, 2, k))
 
     for r in range(2):
         mine = tok.at[r, outer_place(r), inner_place(r)]
@@ -228,22 +231,27 @@
             part[r] = result
         else:
             send_part[r, d - 1] = result.astype(BF16)
-            send(send_part.at[r, d - 1], in1.at[r, d - 1], ("s", name, d), outer_to(r, o))
+            if d == 2:
+                for k in (1, 3, 2, 0):
+                    i = at(inner_place(r), k)
+                    send(send_part.at[r, 1, i], in1.at[r, 1, i], ("s", name, d, k), outer_to(r, o))
+            else:
+                send(send_part.at[r, d - 1], in1.at[r, d - 1], ("s", name, d), outer_to(r, o))
 
     for_pair(0)
+    pass_on(0)
+    pass_on(3)
     for_lanes(0)
-    group_arrived(1)
-    group_arrived(3)
-    share_group(0, 2)
-    share_group(1, 2)
+    pass_on(1)
+    pass_on(2)
     for_pair(1)
     for_pair(3)
     for_lanes(1)
     for_lanes(3)
-    group_arrived(2)
+    opposite_arrived()
     for_pair(2)
+    hidden(1)
     for_lanes(2)
-    hidden(1)
     hidden(3)
     forward(1)
     second(c, 1, "own")
@@ -261,39 +269,49 @@
     second(pair, 0, "pair")
 
     for name, r in (("own", c), ("pair", pair)):
-        for d in (1, 3, 2):
+        for d in (1, 3):
             arrived(in1.at[r, d - 1], ("s", name, d))
-        value = part[r]
-        for d in range(3):
-            value = value + in1[r, d].astype(F32)
-        total[r] = value
-        send_total[r] = value.astype(BF16)
-        for d in (1, 3, 2):
-            i = at(inner_place(r), d)
-            send(send_total.at[r, i], in2.at[r, d - 1], ("S", name, d), inner_to(r, i))
+        for k in (1, 3, 2, 0):
+            i = at(inner_place(r), k)
+            arrived(in1.at[r, 1, i], ("s", name, 2, k))
+            value = part[r, i]
+            for d in range(3):
+                value = value + in1[r, d, i].astype(F32)
+            if k == 0:
+                total[r] = value
+            else:
+                send_total[r, i] = value.astype(BF16)
+                send(send_total.at[r, i], in2.at[r, k - 1], ("S", name, k), inner_to(r, i))
+    from_zh = [number(("Z", d)) for d in range(4)][0]
+    z_sends = []
     for name, r in (("own", c), ("pair", pair)):
         for d in (1, 3, 2):
             arrived(in2.at[r, d - 1], ("S", name, d))
-    for r in range(2):
-        value = total[r, inner_place(r)]
+        value = total[r]
         for d in range(3):
             value = value + in2[r, d].astype(F32)
         for zi in range(2):
+            i = 2 * r + zi
             block = value[20 * zi : 20 * (zi + 1)]
-            z_own[2 * r + zi] = block
-            z_out[2 * r + zi] = pack(block)
+            z_own[i] = block
+            z_out[i] = pack(block)
+            one = pltpu.make_async_remote_copy(
+                src_ref=z_out.at[i], dst_ref=z_in.at[h], send_sem=ss.at[number(("Z", name, zi))],
+                recv_sem=rs.at[from_zh + h], device_id={H: i}, device_id_type=MESH,
+            )
+            z_sends.append((i, one))
+            pl.when(i != h)(one.start)
     for d in (1, 3, 2):
-        i = at(h, d)
-        send(z_out.at[i], z_in.at[d - 1], ("Z", d), {H: i})
-    for d in (1, 3, 2):
-        arrived(z_in.at[d - 1], ("Z", d))
-    value = z_in[0].astype(F32) + z_in[1].astype(F32) + z_in[2].astype(F32)
+        arrived(z_in.at[at(h, d)], from_zh + at(h, d))
+    value = z_in[at(h, 1)].astype(F32) + z_in[at(h, 2)].astype(F32) + z_in[at(h, 3)].astype(F32)
     mine = z_own[h]
     bottom = jnp.concatenate([value[4 * j : 4 * j + 4, WIDTH:] for j in range(3)], axis=1)
     out_ref[...] = (mine + jnp.concatenate([value[:, :WIDTH], bottom], axis=0)).astype(BF16)
 
     for one in sent:
         one.wait_send()
+    for i, one in z_sends:
+        pl.when(i != h)(one.wait_send)
 
 
 def local(tokens, route_ids, route_probs, w_gate, w_up, w_down):
@@ -322,15 +340,15 @@
             pltpu.VMEM((2, 4, PIECE, WIDTH), F32),
             pltpu.VMEM((2, 3, 4, PIECE, WIDTH), BF16),
             pltpu.VMEM((2, 3, 4, PIECE, WIDTH), BF16),
-            pltpu.VMEM((2, 4, PIECE, WIDTH), F32),
+            pltpu.VMEM((2, PIECE, WIDTH), F32),
             pltpu.VMEM((2, 4, PIECE, WIDTH), BF16),
             pltpu.VMEM((2, 3, PIECE, WIDTH), BF16),
             pltpu.VMEM((4, 20, WIDTH), F32),
             pltpu.VMEM((4, 16, 1024), BF16),
-            pltpu.VMEM((3, 16, 1024), BF16),
+            pltpu.VMEM((4, 16, 1024), BF16),
             pltpu.SemaphoreType.DMA((15,)),
-            pltpu.SemaphoreType.DMA((96,)),
-            pltpu.SemaphoreType.DMA((96,)),
+            pltpu.SemaphoreType.DMA((120,)),
+            pltpu.SemaphoreType.DMA((120,)),
         ],
         compiler_params=pltpu.CompilerParams(
             collective_id=0, has_side_effects=True, vmem_limit_bytes=60 * 2**20

time: 89.6 us -> 87.4 us (0.975)
  the two profiles are of different devices: /device:TPU:1 before, /device:TPU:32 now
where the time goes in v4:
time: 87.4 us; the launch traced here: 87.2 us
  Pallas kernels  85.8 us (98%)
  local copies, waits for them, and re-layouts  1.39 us (2%)
    pallas_call x1, Pallas kernels, local(): pl.pallas_call(kernel, out_shape=jax.ShapeDtypeStruct((20, WIDTH), BF16),...  85.8 us

profile of v4, /device:TPU:32, one launch (start us, length us, event | category | flops | bytes accessed | tf_op | source)
XLA Modules:
  0.0 87.2 jit_solution(5187282859037747053)
XLA Ops:
  0.0 85.8 %shard_map.64 = bf16[20,768]{1,0:T(8,128)(2,1)} custom-call(bf16[20,768]{1,0:T(8,128)(2,1)} %tok_hbm.1, s32[2,1280]{1,0:T(2,128)} %bitcast.2, bf16[2,1280]{1,0:T(2,128)(2,1)} %bitcast.3, bf16[4,768,128]{2,1,0:T(8,128)(2,1)} %wg_ref.1, bf16[4,768,128]{2,1,0:T(8,128)(2,1)} %wu_ref.1, bf16[4,128,768]{2,1,0:T(8,128)(2,1)} %wd_ref.1), custom_call_target="tpu_custom_call" | custom-call | tf_op jit(solution)/shard_map/pallas_call | solution.py:319
  85.8 1.4 %copy.8 = bf16[20,768]{1,0:T(8,128)(2,1)} copy(bf16[20,768]{1,0:T(8,128)(2,1)} %shard_map.64) | data formatting | bytes 61440

commit v5 on v4

--- a/solution.py
+++ b/solution.py
@@ -255,13 +255,13 @@
     hidden(3)
     forward(1)
     second(c, 1, "own")
+    hidden(2)
     forward(3)
     second(pair, 1, "pair")
+    hidden(0)
     second(c, 3, "own")
+    forward(2)
     second(pair, 3, "pair")
-    hidden(2)
-    hidden(0)
-    forward(2)
     second(c, 2, "own")
     second(pair, 2, "pair")
     forward(0)

time: 87.4 us -> 85.8 us (0.982)
  the two profiles are of different devices: /device:TPU:32 before, /device:TPU:1 now
where the time goes in v5:
time: 85.8 us; the launch traced here: 84.2 us
  Pallas kernels  82.8 us (97%)
  local copies, waits for them, and re-layouts  1.39 us (2%)
    pallas_call x1, Pallas kernels, local(): pl.pallas_call(kernel, out_shape=jax.ShapeDtypeStruct((20, WIDTH), BF16),...  82.8 us

profile of v5, /device:TPU:1, one launch (start us, length us, event | category | flops | bytes accessed | tf_op | source)
XLA Modules:
  0.0 84.2 jit_solution(9110712034320095403)
XLA Ops:
  0.0 82.8 %shard_map.64 = bf16[20,768]{1,0:T(8,128)(2,1)} custom-call(bf16[20,768]{1,0:T(8,128)(2,1)} %tok_hbm.1, s32[2,1280]{1,0:T(2,128)} %bitcast.2, bf16[2,1280]{1,0:T(2,128)(2,1)} %bitcast.3, bf16[4,768,128]{2,1,0:T(8,128)(2,1)} %wg_ref.1, bf16[4,768,128]{2,1,0:T(8,128)(2,1)} %wu_ref.1, bf16[4,128,768]{2,1,0:T(8,128)(2,1)} %wd_ref.1), custom_call_target="tpu_custom_call" | custom-call | tf_op jit(solution)/shard_map/pallas_call | solution.py:319
  82.9 1.4 %copy.8 = bf16[20,768]{1,0:T(8,128)(2,1)} copy(bf16[20,768]{1,0:T(8,128)(2,1)} %shard_map.64) | data formatting | bytes 61440

commit v6 on v5

--- a/solution.py
+++ b/solution.py
@@ -248,6 +248,7 @@
     for_pair(3)
     for_lanes(1)
     for_lanes(3)
+    hidden(0)
     opposite_arrived()
     for_pair(2)
     hidden(1)
@@ -258,7 +259,6 @@
     hidden(2)
     forward(3)
     second(pair, 1, "pair")
-    hidden(0)
     second(c, 3, "own")
     forward(2)
     second(pair, 3, "pair")

time: 85.8 us -> 88.2 us (1.028)
  the two profiles are of different devices: /device:TPU:1 before, /device:TPU:9 now
where the time goes in v6:
time: 88.2 us; the launch traced here: 88 us
  Pallas kernels  86.6 us (98%)
  local copies, waits for them, and re-layouts  1.39 us (2%)
    pallas_call x1, Pallas kernels, local(): pl.pallas_call(kernel, out_shape=jax.ShapeDtypeStruct((20, WIDTH), BF16),...  86.6 us

profile of v6, /device:TPU:9, one launch (start us, length us, event | category | flops | bytes accessed | tf_op | source)
XLA Modules:
  0.0 88.0 jit_solution(17013407038861340847)
XLA Ops:
  0.0 86.6 %shard_map.64 = bf16[20,768]{1,0:T(8,128)(2,1)} custom-call(bf16[20,768]{1,0:T(8,128)(2,1)} %tok_hbm.1, s32[2,1280]{1,0:T(2,128)} %bitcast.2, bf16[2,1280]{1,0:T(2,128)(2,1)} %bitcast.3, bf16[4,768,128]{2,1,0:T(8,128)(2,1)} %wg_ref.1, bf16[4,768,128]{2,1,0:T(8,128)(2,1)} %wu_ref.1, bf16[4,128,768]{2,1,0:T(8,128)(2,1)} %wd_ref.1), custom_call_target="tpu_custom_call" | custom-call | tf_op jit(solution)/shard_map/pallas_call | solution.py:319
  86.7 1.4 %copy.8 = bf16[20,768]{1,0:T(8,128)(2,1)} copy(bf16[20,768]{1,0:T(8,128)(2,1)} %shard_map.64) | data formatting | bytes 61440

commit v7 on v6

--- a/solution.py
+++ b/solution.py
@@ -248,7 +248,6 @@
     for_pair(3)
     for_lanes(1)
     for_lanes(3)
-    hidden(0)
     opposite_arrived()
     for_pair(2)
     hidden(1)
@@ -261,6 +260,7 @@
     second(pair, 1, "pair")
     second(c, 3, "own")
     forward(2)
+    hidden(0)
     second(pair, 3, "pair")
     second(c, 2, "own")
     second(pair, 2, "pair")

time: 88.2 us -> 85.9 us (0.974)
  the two profiles are of different devices: /device:TPU:9 before, /device:TPU:38 now
where the time goes in v7:
time: 85.9 us; the launch traced here: 85.7 us
  Pallas kernels  84.3 us (98%)
  local copies, waits for them, and re-layouts  1.39 us (2%)
    pallas_call x1, Pallas kernels, local(): pl.pallas_call(kernel, out_shape=jax.ShapeDtypeStruct((20, WIDTH), BF16),...  84.3 us

profile of v7, /device:TPU:38, one launch (start us, length us, event | category | flops | bytes accessed | tf_op | source)
XLA Modules:
  0.0 85.7 jit_solution(8488289061748028162)
XLA Ops:
  0.0 84.3 %shard_map.64 = bf16[20,768]{1,0:T(8,128)(2,1)} custom-call(bf16[20,768]{1,0:T(8,128)(2,1)} %tok_hbm.1, s32[2,1280]{1,0:T(2,128)} %bitcast.2, bf16[2,1280]{1,0:T(2,128)(2,1)} %bitcast.3, bf16[4,768,128]{2,1,0:T(8,128)(2,1)} %wg_ref.1, bf16[4,768,128]{2,1,0:T(8,128)(2,1)} %wu_ref.1, bf16[4,128,768]{2,1,0:T(8,128)(2,1)} %wd_ref.1), custom_call_target="tpu_custom_call" | custom-call | tf_op jit(solution)/shard_map/pallas_call | solution.py:319
  84.4 1.4 %copy.8 = bf16[20,768]{1,0:T(8,128)(2,1)} copy(bf16[20,768]{1,0:T(8,128)(2,1)} %shard_map.64) | data formatting | bytes 61440
